TPU v7x, 128 devices: a whole 4x4x4 slice. The times are simulated.
128 devices in a mesh: section: 16 (over x, y_hi, core), expert: 8 (over z, y_lo).
Axes of the slice: x: 4, y: 4 (y_hi: 2, y_lo: 2; y = y_hi * 2 + y_lo), z: 4, core: 2. Of those that a mesh axis runs over, the one named last changes fastest.
Arguments:
- resid: bfloat16 [768, 6144], P('expert', 'section'), may hold values from -6 to 6
- query: bfloat16 [768, 6144], P('section', 'expert'), may hold values from -300 to 300, as said below
- new_keys: bfloat16 [768, 1024], P('section', 'expert'), may hold values from -6 to 6
- new_values: bfloat16 [768, 1024], P('section', 'expert'), may hold values from -6 to 6
- cache_keys: bfloat16 [128, 1024, 1024], P('section', None, 'expert'), may hold values from -6 to 6
- cache_values: bfloat16 [128, 1024, 1024], P('section', None, 'expert'), may hold values from -6 to 6
- cache_len: int32 [128], P('section'), may hold values from 1 to 1024, as said below
- out_weight: bfloat16 [6144, 6144], P('expert', 'section'), may hold values from -0.078125 to 0.078125
- expert_ids: int32 [768, 2], replicated, may hold values from 0 to 7, all different within a row; in each aligned block of 96 rows (0 to 95, 96 to 191, ...) at most 30 rows name the same one
- gates: float32 [768, 2], P('expert'), may hold values from 0.05 to 0.95, as said below
- w_gate: bfloat16 [8, 6144, 8192], P('expert', None, 'section'), may hold values from -0.078125 to 0.078125
- w_up: bfloat16 [8, 6144, 8192], P('expert', None, 'section'), may hold values from -0.078125 to 0.078125
- w_down: bfloat16 [8, 8192, 6144], P('expert', 'section'), may hold values from -0.0625 to 0.0625
Outputs:
- layer_out: bfloat16 [768, 6144], P('expert', 'section')
Inputs may be any that keep to these rules, and one draw needn't show every extreme that they name: `query`: some queries may be far larger than typical. `cache_len`: at least one request's cache holds all 1024 positions. `expert_ids`: each row names two different experts; in each aligned block of 96 rows no expert is named by more than 30 rows. `gates`: the two gate weights of a row are positive and sum to one.
All inputs are finite; a program needn't handle non-finite values.
Results may differ from a plain program's by a relative error of at most 0.0055.
Values may be sent and summed in bfloat16 or wider, within the bound.
A program may use at most 128 MiB of HBM per device.

v0:
```python
import math

import jax
import jax.numpy as jnp
from jax import lax
from jax.sharding import PartitionSpec as P

HQ = 48
KV = 8
HD = 128
TOP = 2


def attend(query, new_keys, new_values, cache_keys, cache_values, cache_len):
    requests = cache_keys.shape[0]
    cache_size = cache_keys.shape[1]
    kv_heads = cache_keys.shape[2] // HD
    groups = HQ // KV
    drafts = query.shape[0] // requests
    scale = 1.0 / math.sqrt(HD)
    queries = query.reshape(requests, drafts, kv_heads, groups, HD)
    past_k = cache_keys.reshape(requests, cache_size, kv_heads, HD)
    past_v = cache_values.reshape(requests, cache_size, kv_heads, HD)
    new_k = new_keys.reshape(requests, drafts, kv_heads, HD)
    new_v = new_values.reshape(requests, drafts, kv_heads, HD)
    past_scores = (
        jnp.einsum("rdkgh,rckh->rkgdc", queries, past_k, preferred_element_type=jnp.float32) * scale
    )
    valid = jnp.arange(cache_size, dtype=jnp.int32)[None, :] < cache_len[:, None]
    past_scores = jnp.where(valid[:, None, None, None, :], past_scores, -1e30)
    new_scores = (
        jnp.einsum("rdkgh,rekh->rkgde", queries, new_k, preferred_element_type=jnp.float32) * scale
    )
    causal = jnp.arange(drafts)[:, None] >= jnp.arange(drafts)[None, :]
    new_scores = jnp.where(causal[None, None, None], new_scores, -1e30)
    top_score = jnp.maximum(jnp.max(past_scores, axis=-1), jnp.max(new_scores, axis=-1))
    past_exp = jnp.exp(past_scores - top_score[..., None])
    new_exp = jnp.exp(new_scores - top_score[..., None])
    total = jnp.sum(past_exp, axis=-1) + jnp.sum(new_exp, axis=-1)
    past_prob = (past_exp / total[..., None]).astype(jnp.bfloat16)
    new_prob = (new_exp / total[..., None]).astype(jnp.bfloat16)
    mixed = jnp.einsum("rkgdc,rckh->rdkgh", past_prob, past_v, preferred_element_type=jnp.float32)
    mixed = mixed + jnp.einsum(
        "rkgde,rekh->rdkgh", new_prob, new_v, preferred_element_type=jnp.float32
    )
    return mixed.reshape(requests * drafts, kv_heads * groups * HD).astype(jnp.bfloat16)


def slot_ranks(flat, experts):
    onehot = (flat[..., None] == jnp.arange(experts, dtype=jnp.int32)).astype(jnp.int32)
    return jnp.sum((jnp.cumsum(onehot, axis=1) - onehot) * onehot, axis=-1)


def per_device(
    resid,
    query,
    new_keys,
    new_values,
    cache_keys,
    cache_values,
    cache_len,
    out_weight,
    expert_ids,
    gates,
    w_gate,
    w_up,
    w_down,
):
    attended = attend(query, new_keys, new_values, cache_keys, cache_values, cache_len)
    gathered = lax.all_gather(attended, "section", axis=0, tiled=True)
    block_rows = resid.shape[0]
    projected = lax.psum_scatter(
        jnp.dot(gathered, out_weight, preferred_element_type=jnp.float32),
        "expert",
        scatter_dimension=0,
        tiled=True,
    )
    hidden_in = (resid.astype(jnp.float32) + projected).astype(jnp.bfloat16)
    experts = lax.axis_size("expert")
    capacity = (block_rows * TOP * 5 + 4 * experts - 1) // (4 * experts)
    slots_total = experts * capacity
    own_index = lax.axis_index("expert")
    own_ids = lax.dynamic_slice_in_dim(expert_ids, own_index * block_rows, block_rows, 0)
    own_flat = own_ids.reshape(1, block_rows * TOP)
    destination = (own_flat * capacity + slot_ranks(own_flat, experts)).reshape(-1)
    slot_iota = jnp.arange(slots_total, dtype=jnp.int32)[:, None]
    everyone = lax.all_gather(hidden_in, "expert", axis=0, tiled=True)
    flat_all = expert_ids.reshape(experts, block_rows * TOP)
    offsets = jnp.arange(experts, dtype=jnp.int32)[:, None] * capacity
    target = jnp.where(flat_all == own_index, offsets + slot_ranks(flat_all, experts), -1).reshape(
        -1
    )
    picker = (
        (target[None, :] == slot_iota)
        .reshape(slots_total, experts * block_rows, TOP)
        .sum(-1)
        .astype(jnp.bfloat16)
    )
    received = jnp.dot(picker, everyone, preferred_element_type=jnp.float32).astype(jnp.bfloat16)
    gate_local = w_gate[0]
    up_local = w_up[0]
    down_local = w_down[0]
    piece = lax.all_gather(received, "section", axis=1, tiled=True)
    gate_acc = jnp.dot(piece, gate_local, preferred_element_type=jnp.float32)
    up_acc = jnp.dot(piece, up_local, preferred_element_type=jnp.float32)
    activated = (jax.nn.silu(gate_acc) * up_acc).astype(jnp.bfloat16)
    partial_out = jnp.dot(activated, down_local, preferred_element_type=jnp.float32)
    summed = lax.psum_scatter(partial_out, "section", scatter_dimension=1, tiled=True)
    returned = lax.all_to_all(
        summed.reshape(experts, capacity, -1), "expert", split_axis=0, concat_axis=0, tiled=True
    )
    returned = returned.reshape(slots_total, -1)
    picked = returned[destination].reshape(block_rows, TOP, -1)
    mixture = jnp.sum(gates[:, :, None] * picked, axis=1)
    return (hidden_in.astype(jnp.float32) + mixture).astype(jnp.bfloat16)


def solution(mesh):
    in_specs = (
        P("expert", "section"),
        P("section", "expert"),
        P("section", "expert"),
        P("section", "expert"),
        P("section", None, "expert"),
        P("section", None, "expert"),
        P("section"),
        P("expert", "section"),
        P(),
        P("expert", None),
        P("expert", None, "section"),
        P("expert", None, "section"),
        P("expert", "section", None),
    )
    out_specs = P("expert", "section")
    return jax.shard_map(
        per_device, mesh=mesh, in_specs=in_specs, out_specs=out_specs, check_vma=False
    )
```

profile of v0, /device:TPU:0, one launch (start us, length us, event | category | flops | bytes accessed | tf_op | source)
XLA Modules:
  0.0 318.0 jit_solution(14640803563757734485)
XLA Ops:
  6.5 1.1 reshape.305
  7.7 0.7 iota_compare_fusion.3
  8.4 0.7 reshape.330
  9.1 0.9 bitcast_reduce_fusion
  10.1 0.6 fusion.53
  10.6 0.1 fusion.39
  10.7 0.5 copy-done.1
  11.2 0.4 fusion.13
  11.7 0.2 fusion.40
  11.9 2.8 fusion.24
  14.7 0.6 copy.59
  15.4 48.0 %all-gather.3.cloned.1.call-done = bf16[768,768]{1,0:T(8,128)(2,1)} async-done(((bf16[48,768]{1,0:T(8,128)(2,1)}), bf16[768,768]{1,0:T(8,128)(2,1)}) %all-gather.3.cloned.1.call-update) | async-done | bytes 1179664 | tf_op jit(solution)/shard_map/all_gather | solution.py:70
  63.4 3.1 fusion.54
  66.6 0.2 copy.45
  66.8 0.2 eq.75
  67.0 4.5 %reduce-window.14 = s32[8,8,2,128]{3,1,2,0:T(8,128)S(1)} reduce-window(s32[8,8,2,128]{3,1,2,0:T(8,128)S(1)} %convert_bitcast_fusion, s32[]{:T(128)} %constant.11.clone.1), window={size=1x1x1x128 pad=0_0x0_0x0_0x127_0}, to_apply=%region_5.6 | reduce-window | flops 2080768 | bytes 131076 | tf_op jit(solution)/shard_map/reduce-window
  71.6 0.1 slice.26
  71.6 0.2 copy.46
  71.9 0.1 add_bitcast_fusion
  72.0 0.3 reduce_sum.61
  72.4 0.1 copy.48
  72.5 0.1 add.79
  72.6 0.1 add.80
  72.7 0.3 convert_reduce_fusion
  73.0 34.7 %reduce-scatter.3.cloned.1.call-done = f32[96,384]{1,0:T(8,128)} async-done(((f32[768,384]{1,0:T(8,128)}), f32[96,384]{1,0:T(8,128)}) %reduce-scatter.3.cloned.1.call-update) | async-done | bytes 147472 | tf_op jit(solution)/shard_map/reduce_scatter | solution.py:72
  107.7 0.9 add_convert_fusion.1
  108.6 29.5 %all_gather.10 = bf16[768,384]{1,0:T(8,128)(2,1)S(1)} all-gather(bf16[96,384]{1,0:T(8,128)(2,1)S(1)} %add_convert_fusion.1), channel_id=1, replica_groups=mesh['section'=16,'expert'=8] {'expert'}, dimensions={0}, use_global_device_ids=true | all-gather | bytes 663552 | tf_op jit(solution)/shard_map/all_gather | solution.py:87
  138.2 1.0 convolution_convert_fusion
  139.3 52.2 %all-gather.5.cloned.1.call-done = bf16[240,6144]{1,0:T(8,128)(2,1)} async-done(((bf16[240,384]{1,0:T(8,128)(2,1)}), bf16[240,6144]{1,0:T(8,128)(2,1)}) %all-gather.5.cloned.1.call-update) | async-done | bytes 2949136 | tf_op jit(solution)/shard_map/all_gather | solution.py:103
  191.5 5.4 %fusion.4 = f32[240,512]{1,0:T(8,128)S(1)} fusion(bf16[240,6144]{1,0:T(8,128)(2,1)} %all-gather.5.cloned.1.call-done, bf16[1,6144,512]{2,1,0:T(8,128)(2,1)} %param.23), kind=kOutput, calls=%fused_computation.5 | convolution fusion | flops 1509949440 | bytes 9732096 | tf_op jit(solution)/shard_map/dot_general | solution.py:104
  196.9 11.3 %fusion = f32[240,6144]{1,0:T(8,128)} fusion(bf16[1,512,6144]{2,1,0:T(8,128)(2,1)} %param.25, bf16[240,6144]{1,0:T(8,128)(2,1)} %all-gather.5.cloned.1.call-done, bf16[1,6144,512]{2,1,0:T(8,128)(2,1)} %param.24, f32[240,512]{1,0:T(8,128)S(1)} %fusion.4), kind=kOutput, calls=%fused_computation.1 | convolution fusion | flops 3020636160 | bytes 21921792 | tf_op jit(solution)/shard_map/dot_general | solution.py:107
  208.2 0.1 broadcast_multiply_fusion
  208.3 0.1 copy.50
  208.4 0.1 eq.85
  208.5 0.6 reduce-window.16
  209.1 0.2 slice_reduce_fusion
  209.4 0.1 copy.49
  209.5 0.1 mul.88
  209.6 0.1 copy.44
  209.7 0.1 fusion.49
  209.8 85.2 %reduce-scatter.5.cloned.1.call-done = f32[240,384]{1,0:T(8,128)} async-done(((f32[240,6144]{1,0:T(8,128)}), f32[240,384]{1,0:T(8,128)}) %reduce-scatter.5.cloned.1.call-update) | async-done | bytes 368656 | tf_op jit(solution)/shard_map/reduce_scatter | solution.py:108
  295.0 1.8 reshape.312
  296.8 4.5 %all-to-all-start = ((f32[8,30,384]{2,1,0:T(8,128)}), f32[8,30,384]{2,1,0:T(8,128)S(1)}, u32[]{:S(2)}, u32[]{:S(2)}) async-start(f32[8,30,384]{2,1,0:T(8,128)} %reshape.312), calls=%async_computation.2 | async-start | bytes 786432 | tf_op jit(solution)/shard_map/all_to_all | solution.py:109
  301.3 8.0 %all-to-all-done = f32[8,30,384]{2,1,0:T(8,128)S(1)} async-done(((f32[8,30,384]{2,1,0:T(8,128)}), f32[8,30,384]{2,1,0:T(8,128)S(1)}, u32[]{:S(2)}, u32[]{:S(2)}) %all-to-all-start) | async-done | bytes 368672 | tf_op jit(solution)/shard_map/all_to_all | solution.py:109
  309.3 0.9 gather_fusion
  310.2 0.2 reshape.319
  310.4 0.4 multiply_reduce_fusion
  310.8 0.7 add_convert_fusion
  (41 shorter events, 0.5 us)
Async XLA Ops:
  6.5 2.6 copy-start
  6.5 56.9 %all-gather.3.cloned.1.call-start = ((), (), s32[]{:S(2)}) async-start(), calls=%async_computation.3 | async-start | bytes 1253376 | tf_op jit(solution)/shard_map/all_gather | solution.py:70
  10.0 1.2 copy-start.1
  10.1 1.6 copy-start.5
  11.9 51.5 %copy-start.2 = (bf16[768,384]{1,0:T(8,128)(2,1)S(1)}, bf16[768,384]{1,0:T(8,128)(2,1)}, u32[]{:S(2)}) copy-start(bf16[768,384]{1,0:T(8,128)(2,1)} %param.20) | copy-start | bytes 1769476
  15.4 51.2 %copy-start.4 = (s32[768,2]{0,1:T(2,128)S(1)}, s32[768,2]{0,1:T(2,128)}, u32[]{:S(2)}) copy-start(s32[768,2]{0,1:T(2,128)} %param.21) | copy-start | bytes 18436
  15.4 92.3 %reduce-scatter.3.cloned.1.call-start = ((), (), s32[]{:S(2)}) async-start(), calls=%async_computation.4 | async-start | bytes 1327104 | tf_op jit(solution)/shard_map/reduce_scatter | solution.py:72
  66.5 41.2 %copy-start.3 = (bf16[96,384]{1,0:T(8,128)(2,1)S(1)}, bf16[96,384]{1,0:T(8,128)(2,1)}, u32[]{:S(2)}) copy-start(bf16[96,384]{1,0:T(8,128)(2,1)} %param.13) | copy-start | bytes 221188
  66.5 125.0 %all-gather.5.cloned.1.call-start = ((), (), s32[]{:S(2)}) async-start(), calls=%async_computation.5 | async-start | bytes 3133440 | tf_op jit(solution)/shard_map/all_gather | solution.py:103
  139.2 155.8 %reduce-scatter.5.cloned.1.call-start = ((), (), s32[]{:S(2)}) async-start(), calls=%async_computation.6 | async-start | bytes 6266880 | tf_op jit(solution)/shard_map/reduce_scatter | solution.py:108
  208.2 1.5 copy-start.6
  296.8 12.5 %all-to-all-start = ((f32[8,30,384]{2,1,0:T(8,128)}), f32[8,30,384]{2,1,0:T(8,128)S(1)}, u32[]{:S(2)}, u32[]{:S(2)}) async-start(f32[8,30,384]{2,1,0:T(8,128)} %reshape.312), calls=%async_computation.2 | async-start | bytes 786432 | tf_op jit(solution)/shard_map/all_to_all | solution.py:109
Sparse Core Ops, SparseCore 0:
  15.5 47.8 all-gather.2
  66.6 41.0 reduce-scatter.2
  139.4 52.1 all-gather.4
  208.3 86.6 reduce-scatter.4
where the time goes:
time: 318 us
  waiting for transfers between devices  228 us (72%)
  blocking collectives  29.5 us (9%)
  matrix products  25.2 us (8%)
  between operations  13.4 us (4%)
  other arithmetic  9.09 us (3%)
  local copies, waits for them, and re-layouts  7.95 us (2%)
  starting transfers between devices  4.6 us (1%)
    reduce_scatter x1, waiting for transfers between devices, per_device(): lax.psum_scatter(partial_out, 'section', scatter_dimension=1, tiled=True)  85.2 us
    all_gather x1, waiting for transfers between devices, per_device(): piece = lax.all_gather(received, 'section', axis=1, tiled=True)  52.2 us
    all_gather x1, waiting for transfers between devices, per_device(): gathered = lax.all_gather(attended, 'section', axis=0, tiled=True)  48 us
    reduce_scatter x1, waiting for transfers between devices, per_device(): lax.psum_scatter(jnp.dot(gathered, out_weight, preferred_element_type=jnp...  34.7 us
    all_gather x1, blocking collectives, per_device(): everyone = lax.all_gather(hidden_in, 'expert', axis=0, tiled=True)  29.5 us
    dot_general x1, matrix products, per_device(): jnp.dot(activated, down_local, preferred_element_type=jnp.float32)  11.3 us
    all_to_all x1, waiting for transfers between devices, per_device(): lax.all_to_all(summed.reshape(experts, capacity, -1), 'expert', split_axi...  7.96 us
  transfers between devices with their start and end apart: 5, of which 5 were waited for; matrix products, arithmetic and copies ran while one was open for 2% of the time, Pallas kernels for 0%

commit v1 on v0

v1 whole, which is shorter than its diff:
```python
import functools
import math

import jax
import jax.numpy as jnp
import numpy as np
from jax import lax
from jax.experimental import pallas as pl
from jax.experimental.pallas import tpu as pltpu
from jax.sharding import PartitionSpec as P

MESH = pl.DeviceIdType.MESH
BF = jnp.bfloat16
F32 = jnp.float32

GROUPS = 6
HD = 128
DRAFT = 6
REQS = 8
SROWS = 48
PADQ = 48
CACHE = 1024
BLK = 96
CAPP = 32
EXP = 8
CHIPS = 8
SEC = 16
BUF = EXP * CAPP
FEAT = 384
D = 6144
HID = 512
NEG = -1e30


def constants():
    pick = np.zeros((REQS * PADQ, GROUPS * SROWS), np.float32)
    mask = np.zeros((REQS * PADQ, SROWS), np.float32)
    for r in range(REQS):
        for g in range(GROUPS):
            for d in range(DRAFT):
                i = r * PADQ + g * DRAFT + d
                pick[i, g * SROWS + r * DRAFT + d] = 1.0
                mask[i, r * DRAFT : r * DRAFT + d + 1] = 1.0
    return pick, mask


def dot(a, b):
    return jnp.dot(a, b, preferred_element_type=F32)


def dot_t(a, b):
    return lax.dot_general(a, b, (((1,), (1,)), ((), ())), preferred_element_type=F32)


def kernel(
    clen,
    resid_h, query_h, nk_h, nv_h, ck_h, cv_h, ow_h, ids_h, gates_h, wg_h, wu_h, wd_h, pick_h, unpick_h, mask_h,
    out_ref,
    resid, query, nk, nv, ck, cv, ow, ids, gates, wg, wu, wd, pick, unpick, mask,
    qp, snew, att, proj_s, proj_r, hidden, comb, disp_s, big, acc, act,
    pair_s, pair_r, mine, red_s, mid_r, fin_r, ret_s, ret,
    lsem, att_ss, att_rs, proj_ss, proj_rs, disp_ss, disp_rs, big_ss, big_rs,
    pair_ss, pair_rs, red_ss, mid_rs, fin_rs, ret_ss, ret_rs,
):
    s = lax.axis_index("section")
    e = lax.axis_index("expert")
    core = lax.rem(s, 2)
    chip = s // 2
    x, yh = chip // 2, lax.rem(chip, 2)

    def at(dx, dy):
        return lax.rem(x + dx + 4, 4) * 2 + lax.rem(yh + dy, 2)

    def lane(q):
        return (q * 2 + core, e)

    other = (chip * 2 + 1 - core, e)

    loads = [(query_h, query), (pick_h, pick), (nk_h, nk), (mask_h, mask)]
    loads += [(ck_h.at[r], ck.at[r]) for r in range(REQS)]
    loads += [(nv_h, nv)]
    loads += [(cv_h.at[r], cv.at[r]) for r in range(REQS)]
    loads += [(unpick_h, unpick), (ow_h, ow), (ids_h.at[pl.ds(pl.multiple_of(e * BLK, BLK), BLK)], ids)]
    loads += [(gates_h, gates), (resid_h, resid)]
    loads += [(wg_h.at[0], wg), (wu_h.at[0], wu)]
    loads += [(wd_h.at[0, :, pl.ds(q * 2 * FEAT, 2 * FEAT)], wd.at[q]) for q in range(CHIPS)]
    local = [pltpu.make_async_copy(a, b, lsem.at[i]) for i, (a, b) in enumerate(loads)]
    for cp in local:
        cp.start()
    (l_query, l_pick, l_nk, l_mask), l_ck = local[:4], local[4:12]
    l_nv, l_cv = local[12], local[13:21]
    l_unpick, l_ow, l_ids, l_gates, l_resid, l_wg, l_wu = local[21:28]
    l_wd = local[28:36]

    bar = pltpu.get_barrier_semaphore()
    ring = [(1, 0), (3, 0), (2, 0), (0, 1)]
    partners = [lane(at(dx, dy)) for dx, dy in ring] + [other]
    partners += [(s, lax.rem(e + k, EXP)) for k in range(1, EXP)]
    for p in partners:
        pl.semaphore_signal(bar, 1, device_id=p, device_id_type=MESH)

    l_query.wait()
    l_pick.wait()
    stacked = jnp.concatenate([query[:, g * HD : (g + 1) * HD] for g in range(GROUPS)], axis=0)
    qp[...] = dot(pick[...], stacked).astype(BF)
    l_nk.wait()
    l_mask.wait()
    scale = 1.0 / math.sqrt(HD)
    snew[...] = jnp.where(mask[...] > 0.5, dot_t(qp[...], nk[...]) * scale, NEG)
    col = lax.broadcasted_iota(jnp.int32, (PADQ, CACHE), 1)
    l_nv.wait()
    l_unpick.wait()
    mixed = []
    for r in range(REQS):
        l_ck[r].wait()
        rows = pl.ds(r * PADQ, PADQ)
        sc = dot_t(qp[rows, :], ck[r]) * scale
        sc = jnp.where(col < clen[r], sc, NEG)
        sn = snew[rows, :]
        top = jnp.maximum(jnp.max(sc, axis=1, keepdims=True), jnp.max(sn, axis=1, keepdims=True))
        pe = jnp.exp(sc - top)
        ne = jnp.exp(sn - top)
        inv = 1.0 / (jnp.sum(pe, axis=1, keepdims=True) + jnp.sum(ne, axis=1, keepdims=True))
        l_cv[r].wait()
        mixed.append((dot((pe * inv).astype(BF), cv[r]) + dot((ne * inv).astype(BF), nv[...])).astype(BF))
    spread = dot(unpick[...], jnp.concatenate(mixed, axis=0)).astype(BF)
    for g in range(GROUPS):
        att[s, :, g * HD : (g + 1) * HD] = spread[g * SROWS : (g + 1) * SROWS]

    pl.semaphore_wait(bar, len(partners))

    def gather(buf, ss, rs):
        sends = []

        def send(q, dest):
            slot = q * 2 + core
            cp = pltpu.make_async_remote_copy(
                buf.at[slot], buf.at[slot], ss.at[len(sends)], rs.at[slot], device_id=dest, device_id_type=MESH
            )
            cp.start()
            sends.append(cp)

        def arrive(slot):
            pltpu.make_async_remote_copy(
                buf.at[slot], buf.at[slot], ss.at[0], rs.at[slot], device_id=other, device_id_type=MESH
            ).wait_recv()

        def first():
            for d in ((0, 1), (2, 0), (1, 0), (3, 0)):
                send(chip, lane(at(*d)))
            send(chip, other)
            arrive(chip * 2 + 1 - core)

        def mine_in(dx, dy):
            q = at(dx, dy)
            arrive(q * 2 + core)
            if (dx, dy) == (0, 1):
                send(q, lane(at(1, 0)))
                send(q, lane(at(3, 0)))
            if (dx, dy) == (2, 0):
                send(q, lane(at(0, 1)))
            send(q, other)

        def theirs_in(dx, dy):
            arrive(at(dx, dy) * 2 + 1 - core)

        return first, mine_in, theirs_in, sends

    def run_gather(buf, ss, rs, use):
        first, mine_in, theirs_in, sends = gather(buf, ss, rs)
        first()
        use(chip)
        level = ((0, 1), (1, 0), (3, 0), (2, 0))
        for d in level:
            mine_in(*d)
        for d in level:
            theirs_in(*d)
            use(at(*d))
        level = ((1, 1), (3, 1), (2, 1))
        for d in level:
            mine_in(*d)
        for d in level:
            theirs_in(*d)
            use(at(*d))
        return sends

    l_ow.wait()
    pending = []

    def project(q):
        rows = jnp.concatenate([att[q * 2], att[q * 2 + 1]], axis=0)
        proj_s[q] = dot(rows, ow[...]).astype(BF)

        @pl.when(q != e)
        def _():
            pltpu.make_async_remote_copy(
                proj_s.at[q], proj_r.at[e], proj_ss.at[q], proj_rs.at[e], device_id=(s, q), device_id_type=MESH
            ).start()

    pending += run_gather(att, att_ss, att_rs, project)

    l_ids.wait()
    l_gates.wait()
    jv = lax.broadcasted_iota(jnp.int32, (BLK, BUF), 1)
    expert_of = jv // CAPP
    slot_of = lax.rem(jv, CAPP)
    n0 = ids[:, 0:1] == expert_of
    n1 = ids[:, 1:2] == expert_of
    named = jnp.where(n0 | n1, 1.0, 0.0)
    lower = jnp.where(
        lax.broadcasted_iota(jnp.int32, (BLK, BLK), 0) > lax.broadcasted_iota(jnp.int32, (BLK, BLK), 1), 1.0, 0.0
    ).astype(BF)
    earlier = dot(lower, named.astype(BF))
    place = jnp.where(earlier == slot_of.astype(F32), named, 0.0)
    comb[...] = place * (jnp.where(n0, gates[:, 0:1], 0.0) + jnp.where(n1, gates[:, 1:2], 0.0))
    picker = jnp.transpose(place).astype(BF)

    l_resid.wait()
    total = resid[...].astype(F32) + proj_s[e].astype(F32)
    for k in range(1, EXP):
        src = lax.rem(e + k, EXP)
        pltpu.make_async_remote_copy(
            proj_s.at[src], proj_r.at[src], proj_ss.at[src], proj_rs.at[src], device_id=(s, src), device_id_type=MESH
        ).wait_recv()
        total = total + proj_r[src].astype(F32)
    hid = total.astype(BF)
    hidden[...] = hid

    disp_s[...] = dot(picker, hid).astype(BF).reshape(EXP, CAPP, FEAT)
    my_rows = pl.ds(pl.multiple_of(e * CAPP, CAPP), CAPP)
    for k in range(1, EXP):
        d = lax.rem(e + k, EXP)
        cp = pltpu.make_async_remote_copy(
            disp_s.at[d], big.at[s, my_rows], disp_ss.at[k], disp_rs.at[e], device_id=(s, d), device_id_type=MESH
        )
        cp.start()
        pending.append(cp)
    big[s, my_rows, :] = disp_s[e]
    for k in range(1, EXP):
        src = lax.rem(e + k, EXP)
        rows = pl.ds(pl.multiple_of(src * CAPP, CAPP), CAPP)
        pltpu.make_async_remote_copy(
            disp_s.at[src], big.at[s, rows], disp_ss.at[k], disp_rs.at[src], device_id=(s, src), device_id_type=MESH
        ).wait_recv()

    l_wg.wait()
    l_wu.wait()
    done = []

    def up(q):
        rows = jnp.concatenate([big[q * 2], big[q * 2 + 1]], axis=1)
        feats = pl.ds(pl.multiple_of(q * 2 * FEAT, 2 * FEAT), 2 * FEAT)
        ga, ua = dot(rows, wg[feats, :]), dot(rows, wu[feats, :])
        if done:
            acc[0] += ga
            acc[1] += ua
        else:
            acc[0] = ga
            acc[1] = ua
        done.append(q)

    pending += run_gather(big, big_ss, big_rs, up)
    g = acc[0]
    act[...] = (g / (1.0 + jnp.exp(-g)) * acc[1]).astype(BF)

    for cp in l_wd:
        cp.wait()
    order = [(1, 1), (3, 1), (2, 1), (1, 0), (3, 0), (2, 0), (0, 1), (0, 0)]

    def down(i):
        p = dot(act[...], wd[at(*order[i])])
        lo, hi = p[:, :FEAT], p[:, FEAT:]
        mine[i] = jnp.where(core == 0, lo, hi)
        pair_s[i] = jnp.where(core == 0, hi, lo).astype(BF)
        cp = pltpu.make_async_remote_copy(
            pair_s.at[i], pair_r.at[i], pair_ss.at[i], pair_rs.at[i], device_id=other, device_id_type=MESH
        )
        cp.start()
        pending.append(cp)

    def paired(i):
        pltpu.make_async_remote_copy(
            pair_s.at[i], pair_r.at[i], pair_ss.at[i], pair_rs.at[i], device_id=other, device_id_type=MESH
        ).wait_recv()
        return mine[i] + pair_r[i].astype(F32)

    def landed(buf, rs, j):
        pltpu.make_async_remote_copy(
            red_s.at[0], buf.at[j], red_ss.at[0], rs.at[j], device_id=other, device_id_type=MESH
        ).wait_recv()
        return buf[j].astype(F32)

    def push(i, value, dest, buf, rs, j):
        red_s[i] = value.astype(BF)
        cp = pltpu.make_async_remote_copy(
            red_s.at[i], buf.at[j], red_ss.at[i], rs.at[j], device_id=lane(at(*dest)), device_id_type=MESH
        )
        cp.start()
        pending.append(cp)

    def finish(i):
        v = paired(i)
        if i == 0:
            push(0, v, (1, 0), mid_r, mid_rs, 0)
        elif i == 1:
            push(1, v, (3, 0), mid_r, mid_rs, 1)
        elif i == 2:
            push(2, v, (0, 1), mid_r, mid_rs, 2)
        elif i == 3:
            push(3, v, (1, 0), fin_r, fin_rs, 0)
        elif i == 4:
            push(4, v, (3, 0), fin_r, fin_rs, 1)
        elif i == 5:
            push(5, v + landed(mid_r, mid_rs, 2), (2, 0), fin_r, fin_rs, 2)
        elif i == 6:
            push(6, v + landed(mid_r, mid_rs, 0) + landed(mid_r, mid_rs, 1), (0, 1), fin_r, fin_rs, 3)
        else:
            for j in range(4):
                v = v + landed(fin_r, fin_rs, j)
        return v

    down(0)
    for i in range(1, CHIPS):
        down(i)
        finish(i - 1)
    ret_s[...] = finish(CHIPS - 1).astype(BF)

    for k in range(1, EXP):
        d = lax.rem(e + k, EXP)
        rows = pl.ds(pl.multiple_of(d * CAPP, CAPP), CAPP)
        cp = pltpu.make_async_remote_copy(
            ret_s.at[rows], ret.at[my_rows], ret_ss.at[k], ret_rs.at[e], device_id=(s, d), device_id_type=MESH
        )
        cp.start()
        pending.append(cp)
    ret[my_rows, :] = ret_s[my_rows, :]
    w = comb[...]
    w_hi = w.astype(BF)
    w_lo = (w - w_hi.astype(F32)).astype(BF)
    for k in range(1, EXP):
        src = lax.rem(e + k, EXP)
        rows = pl.ds(pl.multiple_of(src * CAPP, CAPP), CAPP)
        pltpu.make_async_remote_copy(
            ret_s.at[rows], ret.at[rows], ret_ss.at[k], ret_rs.at[src], device_id=(s, src), device_id_type=MESH
        ).wait_recv()
    back = ret[...]
    out_ref[...] = (hidden[...].astype(F32) + (dot(w_hi, back) + dot(w_lo, back))).astype(BF)

    for cp in pending:
        cp.wait_send()
    for k in range(1, EXP):
        d = lax.rem(e + k, EXP)
        pltpu.make_async_remote_copy(
            proj_s.at[d], proj_r.at[d], proj_ss.at[d], proj_rs.at[d], device_id=(s, d), device_id_type=MESH
        ).wait_send()


def per_device(
    resid, query, new_keys, new_values, cache_keys, cache_values, cache_len, out_weight,
    expert_ids, gates, w_gate, w_up, w_down,
):
    pick, mask = constants()
    V = pltpu.VMEM
    S = pltpu.SemaphoreType.DMA
    scratch = [
        V((BLK, FEAT), BF), V((SROWS, 768), BF), V((SROWS, HD), BF), V((SROWS, HD), BF),
        V((REQS, CACHE, HD), BF), V((REQS, CACHE, HD), BF), V((768, FEAT), BF),
        V((BLK, 2), jnp.int32), V((BLK, 2), F32),
        V((D, HID), BF), V((D, HID), BF), V((CHIPS, HID, 2 * FEAT), BF),
        V(pick.shape, BF), V(pick.T.shape, BF), V(mask.shape, F32),
        V((REQS * PADQ, HD), BF), V((REQS * PADQ, SROWS), F32),
        V((SEC, SROWS, 768), BF),
        V((EXP, BLK, FEAT), BF), V((EXP, BLK, FEAT), BF),
        V((BLK, FEAT), BF), V((BLK, BUF), F32),
        V((EXP, CAPP, FEAT), BF), V((SEC, BUF, FEAT), BF),
        V((2, BUF, HID), F32), V((BUF, HID), BF),
        V((CHIPS, BUF, FEAT), BF), V((CHIPS, BUF, FEAT), BF), V((CHIPS, BUF, FEAT), F32),
        V((CHIPS, BUF, FEAT), BF), V((3, BUF, FEAT), BF), V((4, BUF, FEAT), BF),
        V((BUF, FEAT), BF), V((BUF, FEAT), BF),
        S((36,)), S((16,)), S((SEC,)), S((EXP,)), S((EXP,)), S((EXP,)), S((EXP,)), S((16,)), S((SEC,)),
        S((CHIPS,)), S((CHIPS,)), S((CHIPS,)), S((3,)), S((4,)), S((EXP,)), S((EXP,)),
    ]
    anyspec = pl.BlockSpec(memory_space=pl.ANY)
    return pl.pallas_call(
        kernel,
        out_shape=jax.ShapeDtypeStruct((BLK, FEAT), BF),
        in_specs=[pl.BlockSpec(memory_space=pltpu.SMEM)] + [anyspec] * 15,
        out_specs=pl.BlockSpec(memory_space=pltpu.VMEM),
        scratch_shapes=scratch,
        compiler_params=pltpu.CompilerParams(collective_id=0, has_side_effects=True, vmem_limit_bytes=60 << 20),
    )(
        cache_len, resid, query, new_keys, new_values, cache_keys, cache_values, out_weight, expert_ids, gates,
        w_gate, w_up, w_down, jnp.asarray(pick, BF), jnp.asarray(pick.T, BF), jnp.asarray(mask, F32),
    )


def solution(mesh):
    in_specs = (
        P("expert", "section"),
        P("section", "expert"),
        P("section", "expert"),
        P("section", "expert"),
        P("section", None, "expert"),
        P("section", None, "expert"),
        P("section"),
        P("expert", "section"),
        P(),
        P("expert", None),
        P("expert", None, "section"),
        P("expert", None, "section"),
        P("expert", "section", None),
    )
    return jax.shard_map(
        per_device, mesh=mesh, in_specs=in_specs, out_specs=P("expert", "section"), check_vma=False
    )
```

time: 318 us -> 84.8 us (0.27)
  waiting for transfers between devices: 228 us -> 0 us
  Pallas kernels: 0 us -> 79.7 us
  blocking collectives: 29.5 us -> 0 us
  matrix products: 25.2 us -> 0 us
  between operations: 13.4 us -> 0.01 us
  other arithmetic: 9.09 us -> 0 us
  starting transfers between devices: 4.6 us -> 0 us
  local copies, waits for them, and re-layouts: 7.95 us -> 4.53 us
    reduce_scatter x2 -> x0, waiting for transfers between devices: 120 us -> none  [the longest x1 85.2 us: per_device(): lax.psum_scatter(partial_out, 'section', scatter_dimension=1, tiled=True)]
    all_gather x2 -> x0, waiting for transfers between devices: 100 us -> none  [the longest x1 52.2 us: per_device(): piece = lax.all_gather(received, 'section', axis=1, tiled=True)]
    pallas_call x0 -> x1, Pallas kernels: none -> 79.7 us  [per_device(): pl.pallas_call(kernel, out_shape=jax.ShapeDtypeStruct((BLK, FEAT), BF), i...]
    all_gather x1 -> x0, blocking collectives: 29.5 us -> none  [per_device(): everyone = lax.all_gather(hidden_in, 'expert', axis=0, tiled=True)]
    dot_general x8 -> x0, matrix products: 25.2 us -> none  [the longest x1 11.3 us: per_device(): jnp.dot(activated, down_local, preferred_element_type=jnp.float32)]
    all_to_all x1 -> x0, waiting for transfers between devices: 7.96 us -> none  [per_device(): lax.all_to_all(summed.reshape(experts, capacity, -1), 'expert', split_axi...]
    another operation x8 -> x0, other arithmetic: 5.37 us -> none
    all_to_all x1 -> x0, starting transfers between devices: 4.47 us -> none  [per_device(): lax.all_to_all(summed.reshape(experts, capacity, -1), 'expert', split_axi...]
  transfers between devices with their start and end apart: 5 -> 0, of which waited for: 5 -> 0; matrix products, arithmetic and copies ran while one was open for 2% -> 0% of each run, Pallas kernels for 0% -> 0%
where the time goes in v1:
time: 84.8 us; the launch traced here: 84.3 us
  Pallas kernels  79.7 us (94%)
  local copies, waits for them, and re-layouts  4.53 us (5%)
    pallas_call x1, Pallas kernels, per_device(): pl.pallas_call(kernel, out_shape=jax.ShapeDtypeStruct((BLK, FEAT), BF), i...  79.7 us
    unnamed x3, local copies, waits for them, and re-layouts  4.53 us

profile of v1, /device:TPU:0, one launch (start us, length us, event | category | flops | bytes accessed | tf_op | source)
XLA Modules:
  0.0 84.3 jit_solution(14632773744155377639)
XLA Ops:
  0.0 1.4 %copy.18.gates_h = f32[96,2]{1,0:T(8,128)} copy(f32[96,2]{0,1:T(2,128)} %param.25) | data formatting | bytes 1536 | tf_op args[9]
  1.4 1.6 %copy.17.ids_h = s32[768,2]{1,0:T(8,128)} copy(s32[768,2]{0,1:T(2,128)} %param.24) | data formatting | bytes 12288 | tf_op args[8]
  3.0 79.7 %shard_map.154 = bf16[96,384]{1,0:T(8,128)(2,1)} custom-call(s32[8]{0:T(128)} %clen.1, bf16[96,384]{1,0:T(8,128)(2,1)} %resid_h.1, bf16[48,768]{1,0:T(8,128)(2,1)} %query_h.1, bf16[48,128]{1,0:T(8,128)(2,1)} %nk_h.1, bf16[48,128]{1,0:T(8,128)(2,1)} %nv_h.1, bf16[8,1024,128]{2,1,0:T(8,128)(2,1)} %ck_h.1, bf16[8,1024,128]{2,1,0:T(8,128)(2,1)} %cv_h.1, ...), custom_call_target="tpu_custom_call" | custom-call | tf_op jit(solution)/shard_map/pallas_call | solution.py:384
  82.7 1.5 %copy.20 = bf16[96,384]{1,0:T(8,128)(2,1)} copy(bf16[96,384]{1,0:T(8,128)(2,1)} %shard_map.154) | data formatting | bytes 147456

commit v2 on v1

v2 whole, which is shorter than its diff:
```python
import functools
import math

import jax
import jax.numpy as jnp
import numpy as np
from jax import lax
from jax.experimental import pallas as pl
from jax.experimental.pallas import tpu as pltpu
from jax.sharding import PartitionSpec as P

MESH = pl.DeviceIdType.MESH
BF = jnp.bfloat16
F32 = jnp.float32

GROUPS = 6
HD = 128
DRAFT = 6
REQS = 8
SROWS = 48
PADQ = 48
CACHE = 1024
BLK = 96
CAPP = 32
EXP = 8
CHIPS = 8
SEC = 16
BUF = EXP * CAPP
FEAT = 384
D = 6144
HID = 512
HALF = BUF // 2
NEG = -1e30
PART, FIRST, HOLD = (32, 16), (0, 32), ((0, 6), (5, 8))
NEAR = [(0, 0), (0, 1), (1, 0), (3, 0), (1, 1), (3, 1), (2, 0), (2, 1)]
ORDER = [(2, 1), (1, 1), (3, 1), (2, 0), (1, 0), (3, 0), (0, 1), (0, 0)]


def constants():
    pick = np.zeros((REQS * PADQ, GROUPS * SROWS), np.float32)
    mask = np.zeros((REQS * PADQ, SROWS), np.float32)
    for r in range(REQS):
        for g in range(GROUPS):
            for d in range(DRAFT):
                i = r * PADQ + g * DRAFT + d
                pick[i, g * SROWS + r * DRAFT + d] = 1.0
                mask[i, r * DRAFT : r * DRAFT + d + 1] = 1.0
    back = []
    for rows, first, (low, high) in zip(PART, FIRST, HOLD):
        cut = pick[low * PADQ : high * PADQ].reshape(-1, GROUPS, SROWS)[:, :, first : first + rows]
        back.append(cut.reshape(-1, GROUPS * rows).T)
    return pick, mask, *back


def dot(a, b):
    return jnp.dot(a, b, preferred_element_type=F32)


def dot_t(a, b):
    return lax.dot_general(a, b, (((1,), (1,)), ((), ())), preferred_element_type=F32)


def kernel(
    clen,
    resid_h, query_h, nk_h, nv_h, ck_h, cv_h, ow_h, ids_h, gates_h, wg_h, wu_h, wd_h, pick_h, back0_h, back1_h, mask_h,
    out_ref,
    resid, query, nk, nv, ck, cv, ow, ids, gates, wg, wu, wd, pick, back0, back1, mask,
    qp, snew, mixed, att0, att1, proj_s0, proj_s1, proj_r0, proj_r1, hidden, picker, comb, disp_s, big, acc, act,
    pair_s, pair_r, mine, red_s, mid_r, hop_r, fin_r, ret_s, ret,
    lsem, ow_ss, ow_rs, att_ss, att_rs, proj_ss, proj_rs, disp_ss, disp_rs, big_ss, big_rs, part_rs,
    pair_ss, pair_rs, red_ss, mid_rs, hop_rs, fin_rs, ret_ss, ret_rs,
):
    s = lax.axis_index("section")
    e = lax.axis_index("expert")
    core = lax.rem(s, 2)
    chip = s // 2
    x, yh = chip // 2, lax.rem(chip, 2)

    def at(dx, dy):
        return lax.rem(x + dx + 4, 4) * 2 + lax.rem(yh + dy, 2)

    def lane(q):
        return (q * 2 + core, e)

    other = (chip * 2 + 1 - core, e)

    loads = [(query_h, query), (pick_h, pick), (nk_h, nk), (mask_h, mask)]
    loads += [(ck_h.at[r], ck.at[r]) for r in range(REQS)]
    loads += [(nv_h, nv)]
    loads += [(cv_h.at[r], cv.at[r]) for r in range(REQS)]
    mine_ow = ow.at[:, pl.ds(pl.multiple_of(core * FEAT, HD), FEAT)]
    loads += [(back0_h, back0), (back1_h, back1), (ow_h, mine_ow), (ids_h, ids), (gates_h, gates), (resid_h, resid)]
    early = len(loads)
    loads += [(wg_h.at[0], wg), (wu_h.at[0], wu)]
    loads += [(wd_h.at[0, :, pl.ds(q * 2 * FEAT, 2 * FEAT)], wd.at[q]) for q in range(CHIPS)]
    local = [pltpu.make_async_copy(a, b, lsem.at[i]) for i, (a, b) in enumerate(loads)]
    for cp in local[:early]:
        cp.start()
    (l_query, l_pick, l_nk, l_mask), l_ck = local[:4], local[4:12]
    l_nv, l_cv = local[12], local[13:21]
    l_back, l_ow, l_ids, l_gates, l_resid, l_wg, l_wu = local[21:23], *local[23:29]
    l_wd = local[29:37]

    bar = pltpu.get_barrier_semaphore()
    ring = [(1, 0), (3, 0), (2, 0), (0, 1)]
    partners = [lane(at(dx, dy)) for dx, dy in ring] + [other]
    partners += [(d, lax.rem(e + k, EXP)) for k in range(1, EXP) for d in (s, other[0])]
    for p in partners:
        pl.semaphore_signal(bar, 1, device_id=p, device_id_type=MESH)

    l_query.wait()
    l_pick.wait()
    stacked = jnp.concatenate([query[:, g * HD : (g + 1) * HD] for g in range(GROUPS)], axis=0)
    qp[...] = dot(pick[...], stacked).astype(BF)
    l_nk.wait()
    l_mask.wait()
    scale = 1.0 / math.sqrt(HD)
    snew[...] = jnp.where(mask[...] > 0.5, dot_t(qp[...], nk[...]) * scale, NEG)
    col = lax.broadcasted_iota(jnp.int32, (PADQ, CACHE), 1)
    l_nv.wait()

    def attend(r):
        l_ck[r].wait()
        rows = pl.ds(r * PADQ, PADQ)
        sc = dot_t(qp[rows, :], ck[r]) * scale
        sc = jnp.where(col < clen[r], sc, NEG)
        sn = snew[rows, :]
        top = jnp.maximum(jnp.max(sc, axis=1, keepdims=True), jnp.max(sn, axis=1, keepdims=True))
        pe = jnp.exp(sc - top)
        ne = jnp.exp(sn - top)
        inv = 1.0 / (jnp.sum(pe, axis=1, keepdims=True) + jnp.sum(ne, axis=1, keepdims=True))
        l_cv[r].wait()
        mixed[rows, :] = (dot((pe * inv).astype(BF), cv[r]) + dot((ne * inv).astype(BF), nv[...])).astype(BF)

    att = (att0, att1)
    pending = []

    def arrive(dst, sem):
        pltpu.make_async_remote_copy(dst, dst, ow_ss, sem, device_id=other, device_id_type=MESH).wait_recv()

    def att_send(h, q, n, dest):
        piece = att[h].at[q]
        cp = pltpu.make_async_remote_copy(
            piece, piece, att_ss.at[h, n], att_rs.at[h, q], device_id=lane(at(*dest)), device_id_type=MESH
        )
        cp.start()
        pending.append(cp)

    def att_start(h):
        l_back[h].wait()
        low, high = HOLD[h]
        spread = dot((back0, back1)[h][...], mixed[low * PADQ : high * PADQ, :]).astype(BF)
        n = PART[h]
        for g in range(GROUPS):
            att[h][chip, :, g * HD : (g + 1) * HD] = spread[g * n : (g + 1) * n]
        for n, d in enumerate(((0, 1), (2, 0), (1, 0), (3, 0))):
            att_send(h, chip, n, d)

    def att_come(h, *d):
        q = at(*d)
        arrive(att[h].at[q], att_rs.at[h, q])
        if d == (0, 1):
            att_send(h, q, 4, (1, 0))
            att_send(h, q, 5, (3, 0))
        if d == (2, 0):
            att_send(h, q, 6, (0, 1))

    for r in range(HOLD[0][1]):
        attend(r)
    pl.semaphore_wait(bar, len(partners))
    l_ow.wait()
    cp = pltpu.make_async_remote_copy(mine_ow, mine_ow, ow_ss, ow_rs, device_id=other, device_id_type=MESH)
    cp.start()
    pending.append(cp)
    att_start(0)
    for r in range(HOLD[0][1], REQS):
        attend(r)
    att_start(1)

    for cp in local[early:]:
        cp.start()
    l_ids.wait()
    l_gates.wait()
    of_block = lax.broadcasted_iota(jnp.int32, (EXP * BLK, BLK), 0) == (
        lax.broadcasted_iota(jnp.int32, (EXP * BLK, BLK), 1) + e * BLK
    )
    named_by = dot(ids[...].astype(F32).astype(BF), jnp.where(of_block, 1.0, 0.0).astype(BF))
    jv = lax.broadcasted_iota(jnp.int32, (BUF, BLK), 0)
    expert_of = (jv // CAPP).astype(F32)
    slot_of = lax.rem(jv, CAPP).astype(F32)
    n0 = named_by[0:1, :] == expert_of
    n1 = named_by[1:2, :] == expert_of
    named = jnp.where(n0 | n1, 1.0, 0.0)
    upper = lax.broadcasted_iota(jnp.int32, (BLK, BLK), 0) < lax.broadcasted_iota(jnp.int32, (BLK, BLK), 1)
    earlier = dot(named.astype(BF), jnp.where(upper, 1.0, 0.0).astype(BF))
    place = jnp.where(earlier == slot_of, named, 0.0)
    picker[...] = place.astype(BF)
    weight = jnp.transpose(place * (jnp.where(n0, gates[0:1, :], 0.0) + jnp.where(n1, gates[1:2, :], 0.0)))
    comb[0] = weight.astype(BF)
    comb[1] = (weight - comb[0].astype(F32)).astype(BF)

    proj_s, proj_r = (proj_s0, proj_s1), (proj_r0, proj_r1)
    their_ow = ow.at[:, pl.ds(pl.multiple_of((1 - core) * FEAT, HD), FEAT)]
    arrive(their_ow, ow_rs)

    def proj_copy(h, q, c, frm):
        return pltpu.make_async_remote_copy(
            proj_s[h].at[q, c], proj_r[h].at[frm, core], proj_ss.at[h, q, c], proj_rs.at[h, frm, core],
            device_id=(chip * 2 + c, q), device_id_type=MESH,
        )

    def project(h, *places):
        chips = [at(*d) for d in places]
        p = dot(jnp.concatenate([att[h][q] for q in chips], axis=0), ow[...]).astype(BF)
        for n, q in enumerate(chips):
            rows = p[n * PART[h] : (n + 1) * PART[h]]
            proj_s[h][q, 0] = rows[:, :FEAT]
            proj_s[h][q, 1] = rows[:, FEAT:]
            proj_copy(h, q, 1 - core, e).start()

            @pl.when(q != e)
            def _():
                proj_copy(h, q, core, e).start()

    project(0, (0, 0))
    project(1, (0, 0))
    for h in range(2):
        att_come(h, 0, 1)
        att_come(h, 2, 0)
        att_come(h, 1, 0)
        att_come(h, 3, 0)
        project(h, (0, 1), (2, 0), (1, 0), (3, 0))
    for h in range(2):
        att_come(h, 1, 1)
        att_come(h, 3, 1)
        att_come(h, 2, 1)
        project(h, (1, 1), (3, 1), (2, 1))

    l_resid.wait()
    total = []
    for h in range(2):
        proj_r[h][e, core] = proj_s[h][e, core]
        for k in range(EXP):
            src = lax.rem(e + k, EXP)
            for c in (1 - core, core)[: 1 if k == 0 else 2]:
                arrive(proj_r[h].at[src, c], proj_rs.at[h, src, c])
    for c in range(2):
        for h in range(2):
            low = c * SROWS + FIRST[h]
            t = resid[low : low + PART[h], :].astype(F32)
            for src in range(EXP):
                t = t + proj_r[h][src, c].astype(F32)
            total.append(t)
    hid = jnp.concatenate(total, axis=0).astype(BF)
    hidden[...] = hid

    z, yl = e // 2, lax.rem(e, 2)

    def block_at(dz, dy):
        return lax.rem(z + dz, 4) * 2 + lax.rem(yl + dy, 2)

    disp_s[...] = dot(picker[...], hid).astype(BF).reshape(EXP, CAPP, FEAT)
    for i in range(1, EXP):
        dz, dy = NEAR[i]
        p = NEAR.index(((4 - dz) % 4, dy))
        d = block_at(dz, dy)
        cp = pltpu.make_async_remote_copy(
            disp_s.at[d], big.at[p // 4, s, pl.ds(p % 4 * CAPP, CAPP)], disp_ss.at[i], disp_rs.at[p],
            device_id=(s, d), device_id_type=MESH,
        )
        cp.start()
        pending.append(cp)
    big[0, s, :CAPP, :] = disp_s[e]

    def dispatched(h):
        for p in range(max(1, h * 4), h * 4 + 4):
            pltpu.make_async_remote_copy(
                disp_s.at[0], big.at[h, s, pl.ds(p % 4 * CAPP, CAPP)], disp_ss.at[0], disp_rs.at[p],
                device_id=(s, block_at(*NEAR[p])), device_id_type=MESH,
            ).wait_recv()

    count = [0]

    def send(src, sem, dest):
        cp = pltpu.make_async_remote_copy(
            src, src, big_ss.at[count[0]], sem, device_id=dest, device_id_type=MESH
        )
        cp.start()
        count[0] += 1
        pending.append(cp)

    def part(h, slot, k):
        return big.at[h, slot, pl.ds(k * HALF // 2, HALF // 2)]

    def start_half(h):
        for d in ((0, 1), (1, 0), (3, 0)):
            send(big.at[h, s], big_rs.at[h, s], lane(at(*d)))
        send(big.at[h, s], big_rs.at[h, s], other)

    def come(h, dx, dy):
        q = at(dx, dy)
        slot = q * 2 + core
        whole = big.at[h, slot]
        if (dx, dy) == (2, 0):
            arrive(part(h, slot, 0), part_rs.at[h, 0])
            arrive(part(h, slot, 1), part_rs.at[h, 1])
            send(whole, big_rs.at[h, slot], lane(at(0, 1)))
        else:
            arrive(whole, big_rs.at[h, slot])
        if (dx, dy) == (0, 1):
            send(whole, big_rs.at[h, slot], lane(at(1, 0)))
            send(whole, big_rs.at[h, slot], lane(at(3, 0)))
        if (dx, dy) == (3, 0):
            send(part(h, slot, 0), part_rs.at[h, 0], lane(at(1, 0)))
        if (dx, dy) == (1, 0):
            send(part(h, slot, 1), part_rs.at[h, 1], lane(at(3, 0)))
        send(whole, big_rs.at[h, slot], other)

    begun = [False, False]

    def up(h, *d):
        q = at(*d)
        theirs = q * 2 + 1 - core
        arrive(big.at[h, theirs], big_rs.at[h, theirs])
        rows = jnp.concatenate([big[h, q * 2], big[h, q * 2 + 1]], axis=1)
        feats = pl.ds(pl.multiple_of(q * 2 * FEAT, 2 * FEAT), 2 * FEAT)
        ga, ua = dot(rows, wg[feats, :]), dot(rows, wu[feats, :])
        if begun[h]:
            acc[h, 0] += ga
            acc[h, 1] += ua
        else:
            acc[h, 0] = ga
            acc[h, 1] = ua
        begun[h] = True

    def activate(h):
        g = acc[h, 0]
        act[h] = (g / (1.0 + jnp.exp(-g)) * acc[h, 1]).astype(BF)

    def down(h, i):
        p = dot(act[h], wd[at(*ORDER[i])])
        lo, hi = p[:, :FEAT], p[:, FEAT:]
        mine[h, i] = jnp.where(core == 0, lo, hi)
        pair_s[h, i] = jnp.where(core == 0, hi, lo).astype(BF)
        cp = pltpu.make_async_remote_copy(
            pair_s.at[h, i], pair_r.at[h, i], pair_ss.at[h, i], pair_rs.at[h, i], device_id=other, device_id_type=MESH
        )
        cp.start()
        pending.append(cp)

    def landed(buf, rs, h, j):
        pltpu.make_async_remote_copy(
            buf.at[h, j], buf.at[h, j], red_ss.at[0, 0], rs.at[h, j], device_id=other, device_id_type=MESH
        ).wait_recv()
        return buf[h, j].astype(F32)

    def push(h, i, src, dst, sem, dest):
        cp = pltpu.make_async_remote_copy(
            src, dst, red_ss.at[h, i], sem, device_id=lane(at(*dest)), device_id_type=MESH
        )
        cp.start()
        pending.append(cp)

    def finish(h, i):
        v = mine[h, i] + landed(pair_r, pair_rs, h, i)
        if i == 3:
            v = v + landed(mid_r, mid_rs, h, 2)
        if i == 6:
            v = v + landed(mid_r, mid_rs, h, 0) + landed(mid_r, mid_rs, h, 1)
        out = red_s.at[h, i]
        if i == 4:
            red_s[h, i, : HALF // 2] = v[: HALF // 2].astype(BF)
            red_s[h, i, HALF // 2 :] = (v[HALF // 2 :] + landed(hop_r, hop_rs, h, 1)).astype(BF)
        elif i == 5:
            red_s[h, i, : HALF // 2] = (v[: HALF // 2] + landed(hop_r, hop_rs, h, 0)).astype(BF)
            red_s[h, i, HALF // 2 :] = v[HALF // 2 :].astype(BF)
        elif i < 7:
            red_s[h, i] = v.astype(BF)
        if i == 0:
            push(h, i, out, mid_r.at[h, 2], mid_rs.at[h, 2], (0, 1))
        elif i == 1:
            push(h, i, out, mid_r.at[h, 0], mid_rs.at[h, 0], (1, 0))
        elif i == 2:
            push(h, i, out, mid_r.at[h, 1], mid_rs.at[h, 1], (3, 0))
        elif i == 3:
            push(h, i, out.at[pl.ds(0, HALF // 2)], hop_r.at[h, 0], hop_rs.at[h, 0], (3, 0))
            push(h, 7, out.at[pl.ds(HALF // 2, HALF // 2)], hop_r.at[h, 1], hop_rs.at[h, 1], (1, 0))
        elif i == 4:
            push(h, i, out, fin_r.at[h, 0], fin_rs.at[h, 0], (1, 0))
        elif i == 5:
            push(h, i, out, fin_r.at[h, 1], fin_rs.at[h, 1], (3, 0))
        elif i == 6:
            push(h, i, out, fin_r.at[h, 2], fin_rs.at[h, 2], (0, 1))
        else:
            for j in range(3):
                v = v + landed(fin_r, fin_rs, h, j)
            ret_s[h] = v.astype(BF)
            for p in range(max(1, h * 4), h * 4 + 4):
                d = block_at(*NEAR[p])
                cp = pltpu.make_async_remote_copy(
                    ret_s.at[h, pl.ds(p % 4 * CAPP, CAPP)], ret.at[e], ret_ss.at[p], ret_rs.at[e],
                    device_id=(s, d), device_id_type=MESH,
                )
                cp.start()
                pending.append(cp)
            if h == 0:
                ret[e] = ret_s[0, :CAPP]

    dispatched(0)
    start_half(0)
    dispatched(1)
    start_half(1)
    l_wg.wait()
    l_wu.wait()
    up(0, 0, 0)
    up(1, 0, 0)
    for h in range(2):
        come(h, 1, 0)
        come(h, 3, 0)
    for h in range(2):
        come(h, 0, 1)
    up(0, 1, 0)
    up(0, 3, 0)
    up(0, 0, 1)
    come(0, 2, 0)
    up(1, 1, 0)
    up(1, 3, 0)
    come(1, 2, 0)
    up(1, 0, 1)
    up(0, 2, 0)
    come(0, 1, 1)
    come(0, 3, 1)
    up(1, 2, 0)
    come(1, 1, 1)
    come(1, 3, 1)
    up(0, 1, 1)
    up(0, 3, 1)
    come(0, 2, 1)
    up(1, 1, 1)
    up(1, 3, 1)
    up(0, 2, 1)
    activate(0)
    for cp in l_wd:
        cp.wait()
    down(0, 0)
    down(0, 1)
    finish(0, 0)
    down(0, 2)
    finish(0, 1)
    finish(0, 2)
    come(1, 2, 1)
    up(1, 2, 1)
    activate(1)
    down(1, 0)
    down(1, 1)
    finish(1, 0)
    down(1, 2)
    finish(1, 1)
    finish(1, 2)
    down(0, 3)
    finish(0, 3)
    down(1, 3)
    down(0, 6)
    down(0, 4)
    down(0, 5)
    finish(1, 3)
    finish(0, 6)
    down(1, 6)
    down(1, 4)
    down(1, 5)
    finish(0, 4)
    finish(0, 5)
    finish(1, 6)
    down(0, 7)
    down(1, 7)
    finish(1, 4)
    finish(1, 5)
    finish(0, 7)
    finish(1, 7)

    for k in range(1, EXP):
        src = lax.rem(e + k, EXP)
        pltpu.make_async_remote_copy(
            ret.at[src], ret.at[src], ret_ss.at[0], ret_rs.at[src], device_id=(s, src), device_id_type=MESH
        ).wait_recv()
    back = ret[...].reshape(BUF, FEAT)
    out_ref[...] = hidden[...].astype(F32) + (dot(comb[0], back) + dot(comb[1], back))

    for cp in pending:
        cp.wait_send()
    for h in range(2):
        for k in range(EXP):
            d = lax.rem(e + k, EXP)
            for c in (1 - core, core)[: 1 if k == 0 else 2]:
                proj_copy(h, d, c, e).wait_send()


def per_device(
    resid, query, new_keys, new_values, cache_keys, cache_values, cache_len, out_weight,
    expert_ids, gates, w_gate, w_up, w_down,
):
    pick, mask, back0, back1 = constants()
    V = pltpu.VMEM
    S = pltpu.SemaphoreType.DMA
    scratch = [
        V((BLK, FEAT), BF), V((SROWS, 768), BF), V((SROWS, HD), BF), V((SROWS, HD), BF),
        V((REQS, CACHE, HD), BF), V((REQS, CACHE, HD), BF), V((768, 2 * FEAT), BF),
        V((2, EXP * BLK), jnp.int32), V((2, BLK), F32),
        V((D, HID), BF), V((D, HID), BF), V((CHIPS, HID, 2 * FEAT), BF),
        V(pick.shape, BF), V(back0.shape, BF), V(back1.shape, BF), V(mask.shape, F32),
        V((REQS * PADQ, HD), BF), V((REQS * PADQ, SROWS), F32),
        V((REQS * PADQ, HD), BF), V((CHIPS, PART[0], 768), BF), V((CHIPS, PART[1], 768), BF),
        V((EXP, 2, PART[0], FEAT), BF), V((EXP, 2, PART[1], FEAT), BF),
        V((EXP, 2, PART[0], FEAT), BF), V((EXP, 2, PART[1], FEAT), BF),
        V((BLK, FEAT), BF), V((BUF, BLK), BF), V((2, BLK, BUF), BF),
        V((EXP, CAPP, FEAT), BF), V((2, SEC, HALF, FEAT), BF),
        V((2, 2, HALF, HID), F32), V((2, HALF, HID), BF),
        V((2, CHIPS, HALF, FEAT), BF), V((2, CHIPS, HALF, FEAT), BF), V((2, CHIPS, HALF, FEAT), F32),
        V((2, CHIPS, HALF, FEAT), BF), V((2, 3, HALF, FEAT), BF),
        V((2, 2, HALF // 2, FEAT), BF), V((2, 3, HALF, FEAT), BF),
        V((2, HALF, FEAT), BF), V((EXP, CAPP, FEAT), BF),
        S((37,)), S, S, S((2, 7)), S((2, CHIPS)), S((2, EXP, 2)), S((2, EXP, 2)), S((EXP,)), S((EXP,)), S((40,)), S((2, SEC)), S((2, 2)),
        S((2, CHIPS)), S((2, CHIPS)), S((2, CHIPS)), S((2, 3)), S((2, 2)), S((2, 3)), S((EXP,)), S((EXP,)),
    ]
    anyspec = pl.BlockSpec(memory_space=pl.ANY)
    out = pl.pallas_call(
        kernel,
        out_shape=jax.ShapeDtypeStruct((BLK, FEAT), F32),
        in_specs=[pl.BlockSpec(memory_space=pltpu.SMEM)] + [anyspec] * 16,
        out_specs=pl.BlockSpec(memory_space=pltpu.VMEM),
        scratch_shapes=scratch,
        compiler_params=pltpu.CompilerParams(collective_id=0, has_side_effects=True, vmem_limit_bytes=60 << 20),
    )(
        cache_len, resid, query, new_keys, new_values, cache_keys, cache_values, out_weight, expert_ids.T, gates.T,
        w_gate, w_up, w_down, jnp.asarray(pick, BF), jnp.asarray(back0, BF), jnp.asarray(back1, BF), jnp.asarray(mask, F32),
    )
    return out.astype(BF)


def solution(mesh):
    in_specs = (
        P("expert", "section"),
        P("section", "expert"),
        P("section", "expert"),
        P("section", "expert"),
        P("section", None, "expert"),
        P("section", None, "expert"),
        P("section"),
        P("expert", "section"),
        P(),
        P("expert", None),
        P("expert", None, "section"),
        P("expert", None, "section"),
        P("expert", "section", None),
    )
    return jax.shard_map(
        per_device, mesh=mesh, in_specs=in_specs, out_specs=P("expert", "section"), check_vma=False
    )
```

time: 84.8 us -> 73.9 us (0.87)
  Pallas kernels: 79.7 us -> 72.3 us
  local copies, waits for them, and re-layouts: 4.53 us -> 0 us
  other arithmetic: 0 us -> 1.55 us
    pallas_call x1, Pallas kernels: 79.7 us -> 72.3 us  [per_device(): pl.pallas_call(kernel, out_shape=jax.ShapeDtypeStruct((BLK, FEAT), F32),...]
    unnamed x3 -> x0, local copies, waits for them, and re-layouts: 4.53 us -> none
    convert_element_type x0 -> x1, other arithmetic: none -> 1.55 us  [per_device(): return out.astype(BF)]
where the time goes in v2:
time: 73.9 us; the launch traced here: 73.8 us
  Pallas kernels  72.3 us (98%)
  other arithmetic  1.55 us (2%)
    pallas_call x1, Pallas kernels, per_device(): pl.pallas_call(kernel, out_shape=jax.ShapeDtypeStruct((BLK, FEAT), F32),...  72.3 us
    convert_element_type x1, other arithmetic, per_device(): return out.astype(BF)  1.55 us

profile of v2, /device:TPU:0, one launch (start us, length us, event | category | flops | bytes accessed | tf_op | source)
XLA Modules:
  0.0 73.8 jit_solution(12079772097273867578)
XLA Ops:
  0.0 72.3 %shard_map.163 = f32[96,384]{1,0:T(8,128)} custom-call(s32[8]{0:T(128)} %clen.1, bf16[96,384]{1,0:T(8,128)(2,1)} %resid_h.1, bf16[48,768]{1,0:T(8,128)(2,1)} %query_h.1, bf16[48,128]{1,0:T(8,128)(2,1)} %nk_h.1, bf16[48,128]{1,0:T(8,128)(2,1)} %nv_h.1, bf16[8,1024,128]{2,1,0:T(8,128)(2,1)} %ck_h.1, bf16[8,1024,128]{2,1,0:T(8,128)(2,1)} %cv_h.1, ...), custom_call_target="tpu_custom_call" | custom-call | tf_op jit(solution)/shard_map/pallas_call | solution.py:526
  72.3 1.6 %convert_element_type.3 = bf16[96,384]{1,0:T(8,128)(2,1)} convert(f32[96,384]{1,0:T(8,128)} %shard_map.163) | non-fusion elementwise | flops 36864 | bytes 221184 | tf_op jit(solution)/shard_map/convert_element_type | solution.py:537

commit v3 on v2

--- a/solution.py
+++ b/solution.py
@@ -30,6 +30,7 @@
 D = 6144
 HID = 512
 HALF = BUF // 2
+QUART = BUF // 4
 NEG = -1e30
 PART, FIRST, HOLD = (32, 16), (0, 32), ((0, 6), (5, 8))
 NEAR = [(0, 0), (0, 1), (1, 0), (3, 0), (1, 1), (3, 1), (2, 0), (2, 1)]
@@ -176,9 +177,47 @@
     for r in range(HOLD[0][1], REQS):
         attend(r)
     att_start(1)
-
     for cp in local[early:]:
         cp.start()
+
+    proj_s, proj_r = (proj_s0, proj_s1), (proj_r0, proj_r1)
+    their_ow = ow.at[:, pl.ds(pl.multiple_of((1 - core) * FEAT, HD), FEAT)]
+    arrive(their_ow, ow_rs)
+
+    def proj_copy(h, q, c, frm):
+        return pltpu.make_async_remote_copy(
+            proj_s[h].at[q, c], proj_r[h].at[frm, core], proj_ss.at[h, q, c], proj_rs.at[h, frm, core],
+            device_id=(chip * 2 + c, q), device_id_type=MESH,
+        )
+
+    def project(h, *places):
+        chips = [at(*d) for d in places]
+        p = dot(jnp.concatenate([att[h][q] for q in chips], axis=0), ow[...]).astype(BF)
+        for n, q in enumerate(chips):
+            rows = p[n * PART[h] : (n + 1) * PART[h]]
+            proj_s[h][q, 0] = rows[:, :FEAT]
+            proj_s[h][q, 1] = rows[:, FEAT:]
+            proj_copy(h, q, 1 - core, e).start()
+
+            @pl.when(q != e)
+            def _():
+                proj_copy(h, q, core, e).start()
+
+    project(0, (0, 0))
+    project(1, (0, 0))
+    for h in range(2):
+        att_come(h, 0, 1)
+        att_come(h, 2, 0)
+    for h in range(2):
+        att_come(h, 1, 0)
+        att_come(h, 3, 0)
+        project(h, (0, 1), (2, 0), (1, 0), (3, 0))
+    for h in range(2):
+        att_come(h, 1, 1)
+        att_come(h, 3, 1)
+        att_come(h, 2, 1)
+        project(h, (1, 1), (3, 1), (2, 1))
+
     l_ids.wait()
     l_gates.wait()
     of_block = lax.broadcasted_iota(jnp.int32, (EXP * BLK, BLK), 0) == (
@@ -199,43 +238,6 @@
     comb[0] = weight.astype(BF)
     comb[1] = (weight - comb[0].astype(F32)).astype(BF)
 
-    proj_s, proj_r = (proj_s0, proj_s1), (proj_r0, proj_r1)
-    their_ow = ow.at[:, pl.ds(pl.multiple_of((1 - core) * FEAT, HD), FEAT)]
-    arrive(their_ow, ow_rs)
-
-    def proj_copy(h, q, c, frm):
-        return pltpu.make_async_remote_copy(
-            proj_s[h].at[q, c], proj_r[h].at[frm, core], proj_ss.at[h, q, c], proj_rs.at[h, frm, core],
-            device_id=(chip * 2 + c, q), device_id_type=MESH,
-        )
-
-    def project(h, *places):
-        chips = [at(*d) for d in places]
-        p = dot(jnp.concatenate([att[h][q] for q in chips], axis=0), ow[...]).astype(BF)
-        for n, q in enumerate(chips):
-            rows = p[n * PART[h] : (n + 1) * PART[h]]
-            proj_s[h][q, 0] = rows[:, :FEAT]
-            proj_s[h][q, 1] = rows[:, FEAT:]
-            proj_copy(h, q, 1 - core, e).start()
-
-            @pl.when(q != e)
-            def _():
-                proj_copy(h, q, core, e).start()
-
-    project(0, (0, 0))
-    project(1, (0, 0))
-    for h in range(2):
-        att_come(h, 0, 1)
-        att_come(h, 2, 0)
-        att_come(h, 1, 0)
-        att_come(h, 3, 0)
-        project(h, (0, 1), (2, 0), (1, 0), (3, 0))
-    for h in range(2):
-        att_come(h, 1, 1)
-        att_come(h, 3, 1)
-        att_come(h, 2, 1)
-        project(h, (1, 1), (3, 1), (2, 1))
-
     l_resid.wait()
     total = []
     for h in range(2):
@@ -272,12 +274,9 @@
         pending.append(cp)
     big[0, s, :CAPP, :] = disp_s[e]
 
-    def dispatched(h):
-        for p in range(max(1, h * 4), h * 4 + 4):
-            pltpu.make_async_remote_copy(
-                disp_s.at[0], big.at[h, s, pl.ds(p % 4 * CAPP, CAPP)], disp_ss.at[0], disp_rs.at[p],
-                device_id=(s, block_at(*NEAR[p])), device_id_type=MESH,
-            ).wait_recv()
+    def dispatched(n):
+        for p in range(max(1, 2 * n), 2 * n + 2):
+            arrive(big.at[p // 4, s, pl.ds(p % 4 * CAPP, CAPP)], disp_rs.at[p])
 
     count = [0]
 
@@ -289,39 +288,42 @@
         count[0] += 1
         pending.append(cp)
 
-    def part(h, slot, k):
-        return big.at[h, slot, pl.ds(k * HALF // 2, HALF // 2)]
-
-    def start_half(h):
-        for d in ((0, 1), (1, 0), (3, 0)):
-            send(big.at[h, s], big_rs.at[h, s], lane(at(*d)))
-        send(big.at[h, s], big_rs.at[h, s], other)
-
-    def come(h, dx, dy):
-        q = at(dx, dy)
+    def piece(n, slot, k=0, rows=QUART):
+        return big.at[n // 2, slot, pl.ds(n % 2 * QUART + k * rows, rows)]
+
+    def start(n):
+        dispatched(n)
+        for d in ((1, 0), (3, 0), (0, 1)):
+            send(piece(n, s), big_rs.at[n, s], lane(at(*d)))
+        send(piece(n, s), big_rs.at[n, s], other)
+
+    def come(n, *d):
+        q = at(*d)
         slot = q * 2 + core
-        whole = big.at[h, slot]
-        if (dx, dy) == (2, 0):
-            arrive(part(h, slot, 0), part_rs.at[h, 0])
-            arrive(part(h, slot, 1), part_rs.at[h, 1])
-            send(whole, big_rs.at[h, slot], lane(at(0, 1)))
+        whole, parts = piece(n, slot), [piece(n, slot, k, QUART // 2) for k in range(2)]
+        sem = big_rs.at[n, slot]
+        if d == (2, 0):
+            arrive(parts[0], part_rs.at[n, 0])
+            arrive(parts[1], part_rs.at[n, 1])
+            send(whole, sem, lane(at(0, 1)))
         else:
-            arrive(whole, big_rs.at[h, slot])
-        if (dx, dy) == (0, 1):
-            send(whole, big_rs.at[h, slot], lane(at(1, 0)))
-            send(whole, big_rs.at[h, slot], lane(at(3, 0)))
-        if (dx, dy) == (3, 0):
-            send(part(h, slot, 0), part_rs.at[h, 0], lane(at(1, 0)))
-        if (dx, dy) == (1, 0):
-            send(part(h, slot, 1), part_rs.at[h, 1], lane(at(3, 0)))
-        send(whole, big_rs.at[h, slot], other)
+            arrive(whole, sem)
+        if d == (0, 1):
+            send(whole, sem, lane(at(1, 0)))
+            send(whole, sem, lane(at(3, 0)))
+        if d == (3, 0):
+            send(parts[0], part_rs.at[n, 0], lane(at(1, 0)))
+        if d == (1, 0):
+            send(parts[1], part_rs.at[n, 1], lane(at(3, 0)))
+        send(whole, sem, other)
 
     begun = [False, False]
 
     def up(h, *d):
         q = at(*d)
         theirs = q * 2 + 1 - core
-        arrive(big.at[h, theirs], big_rs.at[h, theirs])
+        for n in (2 * h, 2 * h + 1):
+            arrive(piece(n, theirs), big_rs.at[n, theirs])
         rows = jnp.concatenate([big[h, q * 2], big[h, q * 2 + 1]], axis=1)
         feats = pl.ds(pl.multiple_of(q * 2 * FEAT, 2 * FEAT), 2 * FEAT)
         ga, ua = dot(rows, wg[feats, :]), dot(rows, wu[feats, :])
@@ -406,38 +408,45 @@
             if h == 0:
                 ret[e] = ret_s[0, :CAPP]
 
-    dispatched(0)
-    start_half(0)
-    dispatched(1)
-    start_half(1)
+    first, second = (0, 1), (2, 3)
+    for n in range(4):
+        start(n)
     l_wg.wait()
     l_wu.wait()
+    for n in first:
+        come(n, 1, 0)
+        come(n, 3, 0)
+    for n in first:
+        come(n, 0, 1)
     up(0, 0, 0)
-    up(1, 0, 0)
-    for h in range(2):
-        come(h, 1, 0)
-        come(h, 3, 0)
-    for h in range(2):
-        come(h, 0, 1)
+    for n in second:
+        come(n, 1, 0)
+        come(n, 3, 0)
     up(0, 1, 0)
     up(0, 3, 0)
     up(0, 0, 1)
-    come(0, 2, 0)
+    for n in first:
+        come(n, 2, 0)
+    for n in second:
+        come(n, 0, 1)
+    up(1, 0, 0)
+    up(0, 2, 0)
+    for n in first:
+        come(n, 1, 1)
+        come(n, 3, 1)
     up(1, 1, 0)
     up(1, 3, 0)
-    come(1, 2, 0)
     up(1, 0, 1)
-    up(0, 2, 0)
-    come(0, 1, 1)
-    come(0, 3, 1)
-    up(1, 2, 0)
-    come(1, 1, 1)
-    come(1, 3, 1)
+    for n in second:
+        come(n, 2, 0)
     up(0, 1, 1)
     up(0, 3, 1)
-    come(0, 2, 1)
-    up(1, 1, 1)
-    up(1, 3, 1)
+    for n in first:
+        come(n, 2, 1)
+    up(1, 2, 0)
+    for n in second:
+        come(n, 1, 1)
+        come(n, 3, 1)
     up(0, 2, 1)
     activate(0)
     for cp in l_wd:
@@ -448,7 +457,10 @@
     down(0, 2)
     finish(0, 1)
     finish(0, 2)
-    come(1, 2, 1)
+    up(1, 1, 1)
+    up(1, 3, 1)
+    for n in second:
+        come(n, 2, 1)
     up(1, 2, 1)
     activate(1)
     down(1, 0)
@@ -519,13 +531,13 @@
         V((2, CHIPS, HALF, FEAT), BF), V((2, 3, HALF, FEAT), BF),
         V((2, 2, HALF // 2, FEAT), BF), V((2, 3, HALF, FEAT), BF),
         V((2, HALF, FEAT), BF), V((EXP, CAPP, FEAT), BF),
-        S((37,)), S, S, S((2, 7)), S((2, CHIPS)), S((2, EXP, 2)), S((2, EXP, 2)), S((EXP,)), S((EXP,)), S((40,)), S((2, SEC)), S((2, 2)),
+        S((37,)), S, S, S((2, 7)), S((2, CHIPS)), S((2, EXP, 2)), S((2, EXP, 2)), S((EXP,)), S((EXP,)), S((80,)), S((4, SEC)), S((4, 2)),
         S((2, CHIPS)), S((2, CHIPS)), S((2, CHIPS)), S((2, 3)), S((2, 2)), S((2, 3)), S((EXP,)), S((EXP,)),
     ]
     anyspec = pl.BlockSpec(memory_space=pl.ANY)
     out = pl.pallas_call(
         kernel,
-        out_shape=jax.ShapeDtypeStruct((BLK, FEAT), F32),
+        out_shape=pltpu.VMEM((BLK, FEAT), F32),
         in_specs=[pl.BlockSpec(memory_space=pltpu.SMEM)] + [anyspec] * 16,
         out_specs=pl.BlockSpec(memory_space=pltpu.VMEM),
         scratch_shapes=scratch,

time: 73.9 us -> 71 us (0.961)
  Pallas kernels: 72.3 us -> 70.3 us
  other arithmetic: 1.55 us -> 0.64 us
    pallas_call x1, Pallas kernels: 72.3 us -> 70.3 us  [per_device(): pl.pallas_call(kernel, out_shape=pltpu.VMEM((BLK, FEAT), F32), in_specs=[...]
    convert_element_type x1, other arithmetic: 1.55 us -> 0.64 us  [per_device(): return out.astype(BF)]
where the time goes in v3:
time: 71 us; the launch traced here: 70.9 us
  Pallas kernels  70.3 us (99%)
    pallas_call x1, Pallas kernels, per_device(): pl.pallas_call(kernel, out_shape=pltpu.VMEM((BLK, FEAT), F32), in_specs=[...  70.3 us

profile of v3, /device:TPU:0, one launch (start us, length us, event | category | flops | bytes accessed | tf_op | source)
XLA Modules:
  0.0 70.9 jit_solution(939257389450945329)
XLA Ops:
  0.0 70.3 %shard_map.163 = f32[96,384]{1,0:T(8,128)S(1)} custom-call(s32[8]{0:T(128)} %clen.1, bf16[96,384]{1,0:T(8,128)(2,1)} %resid_h.1, bf16[48,768]{1,0:T(8,128)(2,1)} %query_h.1, bf16[48,128]{1,0:T(8,128)(2,1)} %nk_h.1, bf16[48,128]{1,0:T(8,128)(2,1)} %nv_h.1, bf16[8,1024,128]{2,1,0:T(8,128)(2,1)} %ck_h.1, bf16[8,1024,128]{2,1,0:T(8,128)(2,1)} %cv_h.1, ...), custom_call_target="tpu_custom_call" | custom-call | tf_op jit(solution)/shard_map/pallas_call | solution.py:538
  70.3 0.6 convert_element_type.3

commit v4 on v3

--- a/solution.py
+++ b/solution.py
@@ -239,21 +239,20 @@
     comb[1] = (weight - comb[0].astype(F32)).astype(BF)
 
     l_resid.wait()
-    total = []
+    hid = [[None, None], [None, None]]
     for h in range(2):
         proj_r[h][e, core] = proj_s[h][e, core]
         for k in range(EXP):
             src = lax.rem(e + k, EXP)
             for c in (1 - core, core)[: 1 if k == 0 else 2]:
                 arrive(proj_r[h].at[src, c], proj_rs.at[h, src, c])
-    for c in range(2):
-        for h in range(2):
+        for c in range(2):
             low = c * SROWS + FIRST[h]
             t = resid[low : low + PART[h], :].astype(F32)
             for src in range(EXP):
                 t = t + proj_r[h][src, c].astype(F32)
-            total.append(t)
-    hid = jnp.concatenate(total, axis=0).astype(BF)
+            hid[c][h] = t
+    hid = jnp.concatenate(hid[0] + hid[1], axis=0).astype(BF)
     hidden[...] = hid
 
     z, yl = e // 2, lax.rem(e, 2)

time: 71 us -> 70.9 us (level)
  no operation moved by 1% of the time
where the time goes in v4:
time: 70.9 us; the launch traced here: 70.8 us
  Pallas kernels  70.2 us (99%)
    pallas_call x1, Pallas kernels, per_device(): pl.pallas_call(kernel, out_shape=pltpu.VMEM((BLK, FEAT), F32), in_specs=[...  70.2 us

profile of v4, /device:TPU:0, one launch (start us, length us, event | category | flops | bytes accessed | tf_op | source)
XLA Modules:
  0.0 70.8 jit_solution(5466455083896394640)
XLA Ops:
  0.0 70.2 %shard_map.163 = f32[96,384]{1,0:T(8,128)S(1)} custom-call(s32[8]{0:T(128)} %clen.1, bf16[96,384]{1,0:T(8,128)(2,1)} %resid_h.1, bf16[48,768]{1,0:T(8,128)(2,1)} %query_h.1, bf16[48,128]{1,0:T(8,128)(2,1)} %nk_h.1, bf16[48,128]{1,0:T(8,128)(2,1)} %nv_h.1, bf16[8,1024,128]{2,1,0:T(8,128)(2,1)} %ck_h.1, bf16[8,1024,128]{2,1,0:T(8,128)(2,1)} %cv_h.1, ...), custom_call_target="tpu_custom_call" | custom-call | tf_op jit(solution)/shard_map/pallas_call | solution.py:537
  70.2 0.6 convert_element_type.3
